TPU v7x, 512 devices: a whole 4x4x16 slice. The times are simulated.
512 devices in a mesh: grp: 16 (over x, y), row: 32 (over z, core).
Axes of the slice: x: 4, y: 4, z: 16, core: 2. Of those that a mesh axis runs over, the one named last changes fastest.
Arguments:
- start_vectors: float32 [64, 524288], P(None, ('grp', 'row'))
- start_directions: float32 [64, 524288], P(None, ('grp', 'row'))
- tiles: bfloat16 [53248, 128, 128], P(('grp', 'row')), may hold values from -0.109375 to 0.109375
- tile_row: int32 [53248], P(('grp', 'row')), may hold values from 0 to 7, as said below
- tile_slot: int32 [53248], P(('grp', 'row')), may hold values from 0 to 103, as said below
- tile_count: int32 [512], P(('grp', 'row')), may hold values from 8 to 100, as said below
- send_row: int32 [32768], P(('grp', 'row')), may hold values from -1 to 7, as said below
- send_grp: int32 [16384], P(('grp', 'row')), may hold values from -1 to 7, as said below
- ritz: float32 [2, 192, 128], replicated, may hold values from -0.4375 to 0.4375
Outputs:
- final_vectors: float32 [64, 524288], P(None, ('grp', 'row'))
- final_directions: float32 [64, 524288], P(None, ('grp', 'row'))
Inputs may be any that keep to these rules, and one draw needn't show every extreme that they name: `tile_row`: own row block that a tile slot adds into. `tile_slot`: index into device d's block table: 8 own row blocks, then 32 * 2 slots from its community (p * 2 + s from row index p), then 16 * 2 slots from other communities (h * 2 + s from community h). Among a device's live tile slots each own block and each filled slot is named exactly once, and no empty slot. A device's live tile slots are its first tile_count entries; the rest are unused. In each community one device has every slot from other devices filled. `send_row`: entry (d * 32 + r) * 2 + s: the own row block that device d sends in slot s to the device of row index r in its community, or -1 for an empty slot. A sender's filled entries to one receiver are distinct and come first; its entries to itself are -1; in each community one device receives all 2 slots from every other member. `send_grp`: entry (d * 16 + h) * 2 + s: the own row block that device d sends in slot s to the device of the same row index in community h, or -1 for an empty slot. Filled entries to one receiver are distinct and come first; entries to its own community are -1; the device that receives all in-community slots also receives all 2 slots from every other community.
All inputs are finite; a program needn't handle non-finite values.
Results may differ from a plain program's by a relative error of at most 0.0032.
Values may be sent and summed in bfloat16 or wider, within the bound.
A program may use at most 64 MiB of HBM per device.

v0:
```python
import jax
import jax.numpy as jnp
from jax import lax
from jax.sharding import PartitionSpec as P

ITERS = 2


def select_blocks(source_blocks, positions):
    chosen = jnp.take(source_blocks, jnp.maximum(positions, 0), axis=1)
    return jnp.where((positions >= 0)[None, :, None], chosen, jnp.zeros((), source_blocks.dtype))


def shards(
    start_vectors,
    start_directions,
    tiles,
    tile_row,
    tile_slot,
    tile_count,
    send_row,
    send_grp,
    ritz,
):
    eigen_count, row_width = start_vectors.shape
    tile_size = tiles.shape[1]
    blocks = row_width // tile_size
    row_devices = lax.axis_size("row")
    total_rows = row_width * row_devices * lax.axis_size("grp")
    slot_total = tile_slot.shape[0]
    active = jnp.arange(slot_total, dtype=jnp.int32) < tile_count[0]
    targets = jnp.arange(blocks, dtype=jnp.int32)
    onehot = jnp.where(active[:, None] & (tile_row[:, None] == targets[None, :]), 1.0, 0.0).astype(
        jnp.float32
    )
    vectors, directions = (start_vectors, start_directions)
    for iteration in range(ITERS):
        rounded = vectors.astype(jnp.bfloat16)
        own_blocks = rounded.reshape(eigen_count, blocks, tile_size)
        near_blocks = lax.all_to_all(
            select_blocks(own_blocks, send_row), "row", split_axis=1, concat_axis=1, tiled=True
        )
        far_blocks = lax.all_to_all(
            select_blocks(own_blocks, send_grp), "grp", split_axis=1, concat_axis=1, tiled=True
        )
        block_table = jnp.concatenate([own_blocks, near_blocks, far_blocks], axis=1)
        picked = jnp.take(block_table, tile_slot, axis=1)
        products = lax.dot_general(
            picked, tiles, (((2,), (2,)), ((1,), (0,))), preferred_element_type=jnp.float32
        )
        affinity = jnp.einsum(
            "tr,tkb->krb", onehot, products, precision=lax.Precision.HIGHEST
        ).reshape(eigen_count, row_width)
        stacked = jnp.concatenate([vectors, affinity, directions], axis=0)
        gram_matrix = (
            lax.psum(jnp.dot(stacked, stacked.T, precision=lax.Precision.HIGHEST), ("grp", "row"))
            / total_rows
        )
        factor = jnp.linalg.cholesky(gram_matrix)
        coeffs = lax.linalg.triangular_solve(
            factor, ritz[iteration], left_side=True, lower=True, transpose_a=True
        )
        update = jnp.dot(coeffs.T, stacked, precision=lax.Precision.HIGHEST)
        vectors, directions = (update[:eigen_count], update[eigen_count:])
    return (vectors, directions)


def solution(mesh):
    in_specs = (
        P(None, ("grp", "row")),
        P(None, ("grp", "row")),
        P(("grp", "row"), None, None),
        P(("grp", "row")),
        P(("grp", "row")),
        P(("grp", "row")),
        P(("grp", "row")),
        P(("grp", "row")),
        P(),
    )
    out_specs = (P(None, ("grp", "row")), P(None, ("grp", "row")))
    return jax.shard_map(shards, mesh=mesh, in_specs=in_specs, out_specs=out_specs, check_vma=False)
```

profile of v0, /device:TPU:1, one launch (start us, length us, event | category | flops | bytes accessed | tf_op | source)
XLA Modules:
  0.0 1255.8 jit_solution(17785646903667311971)
XLA Ops:
  7.2 0.8 broadcast_maximum_fusion
  8.0 0.8 broadcast_compare_fusion.2
  8.8 1.8 convert_bitcast_fusion.1
  10.7 1.4 gather_fusion.1
  12.1 2.0 bitcast_select_fusion.3
  14.1 7.6 all-to-all-start.1
  22.4 1.7 gather_fusion
  24.8 2.5 bitcast_select_fusion.1
  27.3 3.5 all-to-all-done.1
  30.8 18.8 %all-to-all-start = ((bf16[64,64,128]{2,0,1:T(8,128)(2,1)}), bf16[64,64,128]{2,0,1:T(8,128)(2,1)}, u32[]{:S(2)}, u32[]{:S(2)}) async-start(bf16[64,64,128]{2,0,1:T(8,128)(2,1)} %bitcast_select_fusion.1), calls=%async_computation | async-start | bytes 2097152 | tf_op jit(solution)/shard_map/all_to_all | solution.py:40
  51.5 1.3 compare_and_fusion
  52.8 1.6 slice_bitcast_fusion
  54.4 50.9 %all-to-all-done = bf16[64,64,128]{2,0,1:T(8,128)(2,1)} async-done(((bf16[64,64,128]{2,0,1:T(8,128)(2,1)}), bf16[64,64,128]{2,0,1:T(8,128)(2,1)}, u32[]{:S(2)}, u32[]{:S(2)}) %all-to-all-start) | async-done | bytes 1048608 | tf_op jit(solution)/shard_map/all_to_all | solution.py:40
  105.4 2.8 pad_maximum_fusion
  108.2 3.5 gather_fusion.2
  111.6 3.9 fusion.6
  115.5 3.8 fusion.2
  119.4 0.9 copy-done.2
  120.3 1.5 fusion.69
  121.8 443.0 %all-reduce.6.cloned.1.call-done = f32[192,192]{0,1:T(8,128)} async-done(((f32[192,192]{0,1:T(8,128)}), f32[192,192]{0,1:T(8,128)}) %all-reduce.6.cloned.1.call-update) | async-done | bytes 147472 | tf_op jit(solution)/shard_map/psum | solution.py:56
  564.8 1.6 broadcast_multiply_fusion.1
  566.4 1.7 copy.27
  568.2 1.0 fusion.17
  570.5 12.5 cholesky.136
  584.4 11.1 custom-call.13
  595.5 1.6 constant_dynamic-update-slice_fusion.5
  597.1 0.9 convolution_subtract_fusion.3
  598.0 5.8 cholesky.156
  607.1 1.0 select_select_fusion.1
  609.6 21.1 %custom-call.14 = f32[2,128,128]{1,2,0:T(8,128)} custom-call(f32[2,128,128]{2,1,0:T(8,128)} %pad_maximum_fusion.5), custom_call_target="InvertDiagBlocksLowerTriangular" | custom-call | tf_op jit(solution)/shard_map/triangular_solve/custom-call.0 | solution.py:60
  630.6 0.9 fusion.39
  631.6 1.1 convolution_subtract_fusion.1
  632.8 1.0 fusion.27
  633.8 1.8 fusion.18
  636.4 1.4 gather_fusion.4
  637.9 2.0 bitcast_select_fusion.2
  639.8 5.2 all-to-all-start.3
  645.0 1.8 gather_fusion.3
  646.8 2.5 bitcast_select_fusion
  649.3 6.1 all-to-all-done.3
  655.4 8.5 all-to-all-start.2
  664.1 1.9 fusion.68
  666.0 53.7 %all-to-all-done.2 = bf16[64,64,128]{2,0,1:T(8,128)(2,1)} async-done(((bf16[64,64,128]{2,0,1:T(8,128)(2,1)}), bf16[64,64,128]{2,0,1:T(8,128)(2,1)}, u32[]{:S(2)}, u32[]{:S(2)}) %all-to-all-start.2) | async-done | bytes 1048608 | tf_op jit(solution)/shard_map/all_to_all | solution.py:40
  719.7 2.8 pad_maximum_fusion.1
  722.5 3.5 gather_fusion.5
  726.0 3.9 fusion.4
  729.9 3.8 fusion
  734.4 1.5 fusion.15
  735.9 443.2 %all-reduce.8.cloned.1.call-done = f32[192,192]{0,1:T(8,128)} async-done(((f32[192,192]{0,1:T(8,128)}), f32[192,192]{0,1:T(8,128)}) %all-reduce.8.cloned.1.call-update) | async-done | bytes 147472 | tf_op jit(solution)/shard_map/psum | solution.py:56
  1179.2 1.6 broadcast_multiply_fusion
  1180.8 1.7 copy.33
  1182.5 1.0 fusion.16
  1184.9 12.5 cholesky.174
  1198.8 10.8 custom-call.15
  1209.6 1.6 constant_dynamic-update-slice_fusion.3
  1211.1 0.9 convolution_subtract_fusion.2
  1212.1 5.8 cholesky.194
  1221.1 1.0 select_select_fusion
  1222.7 20.3 %custom-call.16 = f32[2,128,128]{1,2,0:T(8,128)} custom-call(f32[2,128,128]{2,1,0:T(8,128)S(1)} %pad_maximum_fusion.6), custom_call_target="InvertDiagBlocksLowerTriangular" | custom-call | tf_op jit(solution)/shard_map/triangular_solve/custom-call.0 | solution.py:60
  1243.0 0.9 fusion.35
  1244.0 1.1 convolution_subtract_fusion
  1245.1 1.0 fusion.25
  1246.2 1.8 fusion.14
  1247.9 0.8 fusion.67
  (94 shorter events, 15.9 us)
Async XLA Ops:
  7.2 104.5 %copy-start = (bf16[104,128,128]{2,1,0:T(8,128)(2,1)S(1)}, bf16[104,128,128]{2,1,0:T(8,128)(2,1)}, u32[]{:S(2)}) copy-start(bf16[104,128,128]{2,1,0:T(8,128)(2,1)} %param.20) | copy-start | bytes 10223620
  8.8 5.3 copy-start.15
  8.8 5.3 copy-start.17
  14.1 16.6 %all-to-all-start.1 = ((bf16[64,32,128]{2,0,1:T(8,128)(2,1)}), bf16[64,32,128]{2,0,1:T(8,128)(2,1)}, u32[]{:S(2)}, u32[]{:S(2)}) async-start(bf16[64,32,128]{2,0,1:T(8,128)(2,1)} %bitcast_select_fusion.3), calls=%async_computation.1 | async-start | bytes 1048576 | tf_op jit(solution)/shard_map/all_to_all | solution.py:43
  22.4 4.8 copy-start.14
  24.8 6.0 copy-start.25
  24.8 6.0 copy-start.27
  30.8 74.6 %all-to-all-start = ((bf16[64,64,128]{2,0,1:T(8,128)(2,1)}), bf16[64,64,128]{2,0,1:T(8,128)(2,1)}, u32[]{:S(2)}, u32[]{:S(2)}) async-start(bf16[64,64,128]{2,0,1:T(8,128)(2,1)} %bitcast_select_fusion.1), calls=%async_computation | async-start | bytes 2097152 | tf_op jit(solution)/shard_map/all_to_all | solution.py:40
  49.6 515.2 %all-reduce.6.cloned.1.call-start = ((), (), s32[]{:S(2)}) async-start(), calls=%async_computation.4 | async-start | bytes 393216 | tf_op jit(solution)/shard_map/psum | solution.py:56
  108.1 3.5 copy-start.23
  111.6 3.9 copy-start.19
  111.6 3.9 copy-start.21
  115.5 3.8 copy-start.1
  115.5 3.8 copy-start.13
  119.4 0.9 copy-start.2
  121.8 509.8 %copy-start.7 = (f32[128,64]{1,0:T(8,128)}, f32[128,64]{1,0:T(8,128)S(1)}, u32[]{:S(2)}) copy-start(f32[128,64]{1,0:T(8,128)S(1)} %pad_convert_fusion) | copy-start | bytes 98308
  569.2 0.7 copy-start.12
  608.1 0.7 copy-start.9
  608.9 29.0 %copy-start.16 = (pred[32]{0:T(512)(128)(4,1)S(1)}, pred[32]{0:T(512)(128)(4,1)}, u32[]{:S(2)}) copy-start(pred[32]{0:T(512)(128)(4,1)} %copy-done.15) | copy-start | bytes 100
  608.9 29.0 %copy-start.18 = (pred[32]{0:T(512)(128)(4,1)S(1)}, pred[32]{0:T(512)(128)(4,1)}, u32[]{:S(2)}) copy-start(pred[32]{0:T(512)(128)(4,1)} %copy-done.17) | copy-start | bytes 100
  635.6 0.8 copy-start.3
  639.8 7.0 copy-start.26
  639.8 7.0 copy-start.28
  639.8 15.5 %all-to-all-start.3 = ((bf16[64,32,128]{2,0,1:T(8,128)(2,1)}), bf16[64,32,128]{2,0,1:T(8,128)(2,1)}, u32[]{:S(2)}, u32[]{:S(2)}) async-start(bf16[64,32,128]{2,0,1:T(8,128)(2,1)} %bitcast_select_fusion.2), calls=%async_computation.3 | async-start | bytes 1048576 | tf_op jit(solution)/shard_map/all_to_all | solution.py:43
  655.4 64.3 %all-to-all-start.2 = ((bf16[64,64,128]{2,0,1:T(8,128)(2,1)}), bf16[64,64,128]{2,0,1:T(8,128)(2,1)}, u32[]{:S(2)}, u32[]{:S(2)}) async-start(bf16[64,64,128]{2,0,1:T(8,128)(2,1)} %bitcast_select_fusion), calls=%async_computation.2 | async-start | bytes 2097152 | tf_op jit(solution)/shard_map/all_to_all | solution.py:40
  663.9 515.2 %all-reduce.8.cloned.1.call-start = ((), (), s32[]{:S(2)}) async-start(), calls=%async_computation.5 | async-start | bytes 393216 | tf_op jit(solution)/shard_map/psum | solution.py:56
  722.5 3.5 copy-start.24
  726.0 3.9 copy-start.20
  726.0 3.9 copy-start.22
  729.9 4.6 copy-start.5
  729.9 4.5 copy-start.6
  733.7 0.7 copy-start.4
  735.9 486.2 %copy-start.8 = (f32[128,64]{1,0:T(8,128)S(1)}, f32[128,64]{1,0:T(8,128)}, u32[]{:S(2)}) copy-start(f32[128,64]{1,0:T(8,128)} %copy-done.7) | copy-start | bytes 98308
  1183.6 0.7 copy-start.11
  1222.0 0.7 copy-start.10
Sparse Core Ops, SparseCore 0:
  121.9 442.8 all-reduce.5
  736.1 443.0 all-reduce.7
where the time goes:
time: 1270 us; the launch traced here: 1260 us
  waiting for transfers between devices  1000 us (79%)
  other arithmetic  135 us (11%)
  starting transfers between devices  40.4 us (3%)
  matrix products  33 us (3%)
  local copies, waits for them, and re-layouts  28.9 us (2%)
  between operations  17.9 us (1%)
    psum x2, waiting for transfers between devices, shards(): lax.psum(jnp.dot(stacked, stacked.T, precision=lax.Precision.HIGHEST), ('...  886 us
    all_to_all x2, waiting for transfers between devices, shards(): lax.all_to_all(select_blocks(own_blocks, send_row), 'row', split_axis=1,...  105 us
    another operation x14, other arithmetic, shards(): factor = jnp.linalg.cholesky(gram_matrix)  63.9 us
    another operation x10, other arithmetic, shards(): lax.linalg.triangular_solve(factor, ritz[iteration], left_side=True, lowe...  44.2 us
    all_to_all x2, starting transfers between devices, shards(): lax.all_to_all(select_blocks(own_blocks, send_row), 'row', split_axis=1,...  27.3 us
  transfers between devices with their start and end apart: 6, of which 6 were waited for; matrix products, arithmetic and copies ran while one was open for 1% of the time, Pallas kernels for 0%

commit v1 on v0

v1 whole, which is shorter than its diff:
```python
import functools

import jax
import jax.numpy as jnp
from jax import lax
from jax.experimental import pallas as pl
from jax.experimental.pallas import tpu as pltpu
from jax.sharding import PartitionSpec as P

ITERS = 2
K = 64
BS = 128
RB = 8
NCH = 2
BPC = RB // NCH
UNROLL = 8
F32, BF16, I32 = jnp.float32, jnp.bfloat16, jnp.int32
MESH = pl.DeviceIdType.MESH
HIGH = lax.Precision.HIGHEST


def dot32(a, b, ca, cb):
    return lax.dot_general(
        a, b, (((ca,), (cb,)), ((), ())), precision=HIGH, preferred_element_type=F32
    )


def dot16(a, b, ca, cb):
    return lax.dot_general(a, b, (((ca,), (cb,)), ((), ())), preferred_element_type=F32)


def split(x):
    hi = x.astype(BF16)
    return hi, (x - hi.astype(F32)).astype(BF16)


def dot3(ah, al, bh, bl, ca, cb):
    return dot16(ah, bh, ca, cb) + (dot16(ah, bl, ca, cb) + dot16(al, bh, ca, cb))


class Eliminate:
    def __init__(self, s, work):
        row = lax.broadcasted_iota(I32, (K, K), 0)
        col = lax.broadcasted_iota(I32, (K, K), 1)
        work[:, 0:K] = s
        work[:, K : 2 * K] = jnp.where(row == col, 1.0, 0.0).astype(F32)
        self.rows = [work[8 * i : 8 * i + 8, :] for i in range(K // 8)]
        self.sub = lax.broadcasted_iota(I32, (8, 2 * K), 0)

    def panel(self, p):
        rows, sub = self.rows, self.sub
        wide = (8, 2 * K)
        cols = [
            [
                jnp.broadcast_to(rows[i][:, 8 * p + k : 8 * p + k + 1], wide)
                for i in range(p, K // 8)
            ]
            for k in range(8)
        ]
        for k in range(8):
            inv = lax.rsqrt(jnp.broadcast_to(cols[k][0][k : k + 1, :], wide))
            low = [c * inv for c in cols[k]]
            for j in range(k + 1, 8):
                mult = jnp.broadcast_to(low[0][j : j + 1, :], wide)
                cols[j] = [c - x * mult for c, x in zip(cols[j], low)]
            pivot = jnp.broadcast_to(rows[p][k : k + 1, :], wide) * inv
            below = jnp.where(sub > k, low[0], 0.0)
            rows[p] = jnp.where(sub == k, pivot, rows[p] - below * pivot)
            for i in range(p + 1, K // 8):
                rows[i] = rows[i] - low[i - p] * pivot

    def inverse(self):
        return jnp.concatenate([r[:, K : 2 * K] for r in self.rows], axis=0)


def kernel(
    ng, nz, total_rows, slots,
    sv, sd, tiles, meta, count, send_row, send_grp, ritz,
    out_v, out_d,
    blk, pack, own, tl, runs, sh, sl, iv, ov, sm_iv, sm_ix, mytb, tb, tv, sm_tv,
    pay, rsb, zb, res, work,
    loc_sem, ring_s, ring_r, sib_s, sib_r, far_s, far_r, tb_s, tb_r, tbx_s, tbx_r,
    rs_s, rs_r, z_s, z_r, ag_s, ag_r,
):
    hops = nz // 2
    far0 = 2 * nz * RB
    pieces = 12 if ng >= 12 else 3
    prow = 96 // pieces
    g, r = lax.axis_index("grp"), lax.axis_index("row")
    z, c = r // 2, r % 2
    m = g * 2 + c
    sib = (g, z * 2 + (1 - c))

    def remote(src, dst, ss, rs, dev):
        return pltpu.make_async_remote_copy(
            src_ref=src, dst_ref=dst, send_sem=ss, recv_sem=rs, device_id=dev, device_id_type=MESH
        )

    def loop(n, body):
        def step(i, carry):
            body(i)
            return carry

        lax.fori_loop(0, n, step, 0)

    def plane_dev(i):
        return (i // 2, z * 2 + i % 2)

    barrier = pltpu.get_barrier_semaphore()

    def greet_z(i):
        @pl.when(i != z)
        def _():
            pl.semaphore_signal(barrier, inc=1, device_id=(g, i * 2 + c), device_id_type=MESH)

    def greet_plane(i):
        @pl.when(i != m)
        def _():
            pl.semaphore_signal(barrier, inc=1, device_id=plane_dev(i), device_id_type=MESH)

    loop(nz, greet_z)
    loop(2 * ng, greet_plane)

    tile_load = pltpu.make_async_copy(tiles, tl, loc_sem.at[0])
    tile_load.start()

    def put_vectors(it):
        for b in range(RB):
            x = sh[0:K, b * BS : (b + 1) * BS]
            own[b] = x
            blk[it, r * RB + b] = x

        def fill(h):
            for s in range(2):
                q = jnp.clip(send_grp[h * 2 + s], 0, RB - 1)
                pack[it, h * 2 + s] = own[q]

        loop(ng, fill)
        zero = jnp.zeros((K, BS), BF16)
        blk[it, far0 + 2 * g] = zero
        blk[it, far0 + 2 * g + 1] = zero

    def split_into(row0, x):
        hi, lo = split(x)
        sh[row0 : row0 + K, :] = hi
        sl[row0 : row0 + K, :] = lo

    split_into(0, sv[...])
    split_into(K, sd[...])
    put_vectors(0)
    mytb[...] = jnp.zeros((8, 128), I32)
    mytb[0:1, 0 : 4 * nz] = send_row[...]
    tb[c, z] = mytb[...]

    pl.semaphore_wait(barrier, nz - 1 + 2 * ng - 1)

    def chunk(it, src_z, core, j, n=BPC):
        return blk.at[it, pl.ds((src_z * 2 + core) * RB + j * BPC, n)]

    def ring_src(d, hop):
        return lax.rem(z + nz - (hop - 1), nz) if d == 0 else lax.rem(z + hop - 1, nz)

    def ring_copy(it, d, hop, j):
        ref = chunk(it, ring_src(d, hop), c, j)
        to = lax.rem(z + 1, nz) if d == 0 else lax.rem(z + nz - 1, nz)
        return remote(ref, ref, ring_s.at[it, d, hop - 1, j], ring_r.at[it, d, hop - 1, j], (g, to * 2 + c))

    def ring_here(it, d, hop, j):
        ref = chunk(it, ring_src(d, hop + 1), c, j)
        return remote(ref, ref, ring_s.at[it, d, hop - 1, j], ring_r.at[it, d, hop - 1, j], sib)

    def sib_copy(it, d, hop, j):
        ref = chunk(it, ring_src(d, hop + 1), c, j)
        return remote(ref, ref, sib_s.at[it, d, hop, j], sib_r.at[it, d, hop, j], sib)

    def sib_here(it, d, hop, j):
        ref = chunk(it, ring_src(d, hop + 1), 1 - c, j)
        return remote(ref, ref, sib_s.at[it, d, hop, j], sib_r.at[it, d, hop, j], sib)

    def ring_parts(hop):
        return [
            (d, j)
            for j in range(NCH)
            for d in range(2)
            if hop < hops or (j < NCH // 2) == (d == 0)
        ]

    def own_to_sib(it, core):
        ref = chunk(it, z, core, 0, RB)
        return remote(ref, ref, sib_s.at[it, 0, 0, 0], sib_r.at[it, 0, 0, 0], sib)

    def far_copy(it, h):
        return remote(
            pack.at[it, pl.ds(h * 2, 2)], blk.at[it, pl.ds(far0 + 2 * g, 2)],
            far_s.at[it, h], far_r.at[it, g], (h, r),
        )

    def far_here(it, h):
        return remote(
            pack.at[it, pl.ds(h * 2, 2)], blk.at[it, pl.ds(far0 + 2 * h, 2)],
            far_s.at[it, h], far_r.at[it, h], (h, r),
        )

    def start_exchange(it):
        for d, j in ring_parts(1):
            ring_copy(it, d, 1, j).start()
        own_to_sib(it, c).start()

        def far(h):
            @pl.when(h != g)
            def _():
                far_copy(it, h).start()

        loop(ng, far)

    def ring_step(it, hop):
        for d, j in ring_parts(hop):
            ring_here(it, d, hop, j).wait_recv()
            if hop < hops and (d, j) in ring_parts(hop + 1):
                ring_copy(it, d, hop + 1, j).start()
            sib_copy(it, d, hop, j).start()

    def finish_exchange(it):
        own_to_sib(it, 1 - c).wait_recv()
        for hop in range(1, hops + 1):
            for d, j in ring_parts(hop):
                sib_here(it, d, hop, j).wait_recv()

        def far(h):
            @pl.when(h != g)
            def _():
                far_here(it, h).wait_recv()

        loop(ng, far)

    def drain_exchange(it):
        own_to_sib(it, c).wait_send()
        for hop in range(1, hops + 1):
            for d, j in ring_parts(hop):
                ring_copy(it, d, hop, j).wait_send()
                sib_copy(it, d, hop, j).wait_send()

        def far(h):
            @pl.when(h != g)
            def _():
                far_copy(it, h).wait_send()

        loop(ng, far)

    def tb_copy(i):
        return remote(mytb, tb.at[c, z], tb_s.at[i], tb_r.at[z], (g, i * 2 + c))

    def tb_here(i):
        return remote(mytb, tb.at[c, i], tb_s.at[i], tb_r.at[i], (g, i * 2 + c))

    def tbx(core):
        return remote(tb.at[core], tb.at[core], tbx_s.at[0], tbx_r.at[0], sib)

    def others(n, me, body):
        def step(i):
            @pl.when(i != me)
            def _():
                body(i)

        loop(n, step)

    owner = (g < pieces) & (c == lax.rem(g, 2))
    mine = pl.ds(pl.multiple_of(lax.rem(g, pieces) * prow, 8), prow)

    def piece(j):
        return pl.ds(pl.multiple_of(j * prow, 8), prow)

    def rs_copy(k, j):
        return remote(pay.at[k, piece(j)], rsb.at[k, m], rs_s.at[k, j], rs_r.at[k, m], (j, z * 2 + lax.rem(j, 2)))

    def rs_here(k, i):
        return remote(pay.at[k, mine], rsb.at[k, i], rs_s.at[k, 0], rs_r.at[k, i], sib)

    def z_copy(k, i):
        return remote(zb.at[k, z], zb.at[k, z], z_s.at[k, i], z_r.at[k, z], (g, i * 2 + c))

    def z_here(k, i):
        return remote(zb.at[k, i], zb.at[k, i], z_s.at[k, i], z_r.at[k, i], sib)

    def ag_copy(k, i):
        return remote(res.at[k, mine], res.at[k, mine], ag_s.at[k, i], ag_r.at[k, lax.rem(g, pieces)], plane_dev(i))

    def ag_here(k, j):
        return remote(res.at[k, piece(j)], res.at[k, piece(j)], ag_s.at[k, j], ag_r.at[k, j], sib)

    def is_mine(j):
        return (g == j) & (c == lax.rem(j, 2))

    def sum_start(k):
        def step(j):
            @pl.when(is_mine(j))
            def _():
                rsb[k, m] = pay[k, piece(j)]

            @pl.when(jnp.logical_not(is_mine(j)))
            def _():
                rs_copy(k, j).start()

        loop(pieces, step)

    def sum_plane(k):
        @pl.when(owner)
        def _():
            others(2 * ng, m, lambda i: rs_here(k, i).wait_recv())
            zb[k, z] = functools.reduce(jnp.add, [rsb[k, i] for i in range(2 * ng)])
            others(nz, z, lambda i: z_copy(k, i).start())

    def sum_z(k):
        @pl.when(owner)
        def _():
            others(nz, z, lambda i: z_here(k, i).wait_recv())
            res[k, mine] = functools.reduce(jnp.add, [zb[k, i] for i in range(nz)])
            others(2 * ng, m, lambda i: ag_copy(k, i).start())

    def sum_end(k):
        def step(j):
            @pl.when(jnp.logical_not(is_mine(j)))
            def _():
                ag_here(k, j).wait_recv()

        loop(pieces, step)

    def sum_drain(k):
        def step(j):
            @pl.when(jnp.logical_not(is_mine(j)))
            def _():
                rs_copy(k, j).wait_send()

        loop(pieces, step)

        @pl.when(owner)
        def _():
            others(nz, z, lambda i: z_copy(k, i).wait_send())
            others(2 * ng, m, lambda i: ag_copy(k, i).wait_send())

    def put_sums(k, wide, square):
        pay[k, 0:K, :] = wide
        pay[k, K : K + K // 2, 0:K] = square[0 : K // 2]
        pay[k, K : K + K // 2, K : 2 * K] = square[K // 2 : K]

    def get_sums(k):
        scale = 1.0 / total_rows
        left = res[k, 0:K, 0:K] * scale
        right = res[k, 0:K, K : 2 * K] * scale
        square = jnp.concatenate(
            [res[k, K : K + K // 2, 0:K], res[k, K : K + K // 2, K : 2 * K]], axis=0
        )
        return left, right, square * scale

    def order_tiles():
        iv[...] = jnp.zeros((8, 128), I32)
        iv[0:2, 0:slots] = meta[...]
        lane = lax.broadcasted_iota(I32, (128, 128), 1)
        subl = lax.broadcasted_iota(I32, (128, 128), 0)
        row_r = jnp.broadcast_to(iv[0:1, :], (128, 128))
        slot_r = jnp.broadcast_to(iv[1:2, :], (128, 128))
        key_r = jnp.where(lane < count[0], row_r * 128 + lane, 2048 + lane)
        row_c, slot_c, key_c = row_r.T, slot_r.T, key_r.T
        rank_r = jnp.sum(jnp.where(key_c < key_r, 1, 0), axis=0, keepdims=True)
        hit = jnp.broadcast_to(rank_r, (128, 128)).T == lane
        tile_at = jnp.sum(jnp.where(hit, subl, 0), axis=0, keepdims=True)
        slot_at = jnp.sum(jnp.where(hit, slot_c, 0), axis=0, keepdims=True)
        row_at = jnp.sum(jnp.where(hit, row_c, 0), axis=0, keepdims=True)
        upto = jnp.where((key_c < 2048) & (row_c <= lane), 1, 0)
        end_at = jnp.sum(upto, axis=0, keepdims=True)
        ov[...] = jnp.zeros((8, 128), I32)
        for i, x in enumerate((tile_at, slot_at, row_at, end_at)):
            ov[i : i + 1, :] = x
        cp = pltpu.make_async_copy(ov, sm_iv, loc_sem.at[1])
        cp.start()
        cp.wait()

    def read_tables():
        tbx(1 - c).wait_recv()
        for i in range(2 * nz):
            tv[i : i + 1, :] = tb[i % 2, i // 2, 0:1, :]
        cp = pltpu.make_async_copy(tv, sm_tv, loc_sem.at[2])
        cp.start()
        cp.wait()

        def step(i):
            e = jnp.clip(sm_iv[1, i], 0, RB + 4 * nz + 2 * ng - 1)
            p = jnp.clip((e - RB) // 2, 0, 2 * nz - 1)
            q = jnp.clip(sm_tv[p, 2 * r + e % 2], 0, RB - 1)
            near = p * RB + q
            far = far0 + jnp.clip(e - RB - 4 * nz, 0, 2 * ng - 1)
            sm_ix[i] = jnp.where(e < RB, r * RB + e, jnp.where(e < RB + 4 * nz, near, far))

        loop(slots, step)

    def tile_products(it):
        def step(k, carry):
            acc, prev = carry
            for u in range(UNROLL):
                i = k * UNROLL + u
                row = sm_iv[2, i]
                keep = jnp.where(row == prev, 1.0, 0.0).astype(F32)
                acc = acc * keep + dot16(blk[it, sm_ix[i]], tl[jnp.clip(sm_iv[0, i], 0, slots - 1)], 1, 1)
                runs[i] = acc
                prev = row
            return acc, prev

        lax.fori_loop(0, slots // UNROLL, step, (jnp.zeros((K, BS), F32), jnp.int32(-1)))
        for b in range(RB):
            end = sm_iv[3, b]
            before = sm_iv[3, b - 1] if b else jnp.int32(0)
            some = jnp.where(end > before, 1.0, 0.0).astype(F32)
            hi, lo = split(runs[jnp.clip(end - 1, 0, slots - 1)] * some)
            sh[2 * K : 3 * K, b * BS : (b + 1) * BS] = hi
            sl[2 * K : 3 * K, b * BS : (b + 1) * BS] = lo

    for it in range(ITERS):
        k0, k1 = 2 * it, 2 * it + 1
        if it:
            put_vectors(it)
        start_exchange(it)
        if it == 0:
            others(nz, z, lambda i: tb_copy(i).start())
        put_sums(
            k0,
            dot3(sh[0:K], sl[0:K], sh[0 : 2 * K], sl[0 : 2 * K], 1, 1),
            dot3(sh[K : 2 * K], sl[K : 2 * K], sh[K : 2 * K], sl[K : 2 * K], 1, 1),
        )
        sum_start(k0)
        state = {}
        for hop in range(1, hops + 1):
            ring_step(it, hop)
            if hop == 1:
                sum_plane(k0)
                if it == 0:
                    order_tiles()
            if hop == 2:
                sum_z(k0)
                if it == 0:
                    others(nz, z, lambda i: tb_here(i).wait_recv())
                    tbx(c).start()
        sum_end(k0)
        if it == 0:
            read_tables()
            tile_load.wait()
        g_vv, g_vd, g_dd = get_sums(k0)
        elim = Eliminate(g_vv, work)
        for p in range(K // 8):
            elim.panel(p)
        e_v = elim.inverse()
        u_d = dot32(e_v, g_vd, 1, 0)
        s_dd = g_dd - dot32(u_d, u_d, 0, 0)

        finish_exchange(it)
        tile_products(it)
        put_sums(
            k1,
            dot3(sh[2 * K : 3 * K], sl[2 * K : 3 * K], sh[0 : 2 * K], sl[0 : 2 * K], 1, 1),
            dot3(sh[2 * K : 3 * K], sl[2 * K : 3 * K], sh[2 * K : 3 * K], sl[2 * K : 3 * K], 1, 1),
        )
        sum_start(k1)
        sum_plane(k1)
        sum_z(k1)
        sum_end(k1)
        g_av, g_ad, g_aa = get_sums(k1)
        u_a = dot32(e_v, g_av, 1, 1)
        s_aa = g_aa - dot32(u_a, u_a, 0, 0)
        s_ad = g_ad - dot32(u_a, u_d, 0, 0)
        elim = Eliminate(s_aa, work)
        for p in range(K // 8):
            elim.panel(p)
        e_a = elim.inverse()
        u_ad = dot32(e_a, s_ad, 1, 0)
        elim = Eliminate(s_dd - dot32(u_ad, u_ad, 0, 0), work)
        for p in range(K // 8):
            elim.panel(p)
        e_d = elim.inverse()
        a_v = -dot32(e_a, dot32(u_a, e_v, 0, 0), 1, 0)
        d_v = -dot32(e_d, dot32(u_d, e_v, 0, 0) + dot32(u_ad, a_v, 0, 0), 1, 0)
        d_a = -dot32(e_d, dot32(u_ad, e_a, 0, 0), 1, 0)
        rz_v, rz_a, rz_d = (ritz[it, i * K : (i + 1) * K, :] for i in range(3))
        c_v = dot32(rz_v, e_v, 0, 0) + dot32(rz_a, a_v, 0, 0) + dot32(rz_d, d_v, 0, 0)
        c_a = dot32(rz_a, e_a, 0, 0) + dot32(rz_d, d_a, 0, 0)
        c_d = dot32(rz_d, e_d, 0, 0)
        ch, cl = split(jnp.concatenate([c_v, c_d, c_a], axis=1))
        new = dot3(ch, cl, sh[...], sl[...], 1, 0)
        if it + 1 < ITERS:
            split_into(0, new[0:K])
            split_into(K, new[K : 2 * K])
        else:
            out_v[...] = new[0:K]
            out_d[...] = new[K : 2 * K]

    others(nz, z, lambda i: tb_copy(i).wait_send())
    tbx(c).wait_send()
    for it in range(ITERS):
        drain_exchange(it)
    for k in range(2 * ITERS):
        sum_drain(k)


def shards(ng, nr, sv, sd, tiles, tile_row, tile_slot, tile_count, send_row, send_grp, ritz):
    nz = nr // 2
    slots = tiles.shape[0]
    width = sv.shape[1]
    nblk = 2 * nz * RB + 2 * ng
    hops = nz // 2
    pieces = 12 if ng >= 12 else 3
    prow = 96 // pieces
    calls = 2 * ITERS
    dma = pltpu.SemaphoreType.DMA
    vmem, smem = pl.BlockSpec(memory_space=pltpu.VMEM), pl.BlockSpec(memory_space=pltpu.SMEM)
    return pl.pallas_call(
        functools.partial(kernel, ng, nz, width * ng * nr, slots),
        out_shape=[jax.ShapeDtypeStruct(sv.shape, F32)] * 2,
        in_specs=[vmem, vmem, pl.BlockSpec(memory_space=pl.ANY), vmem, smem, vmem, smem, vmem],
        out_specs=[vmem, vmem],
        scratch_shapes=[
            pltpu.VMEM((ITERS, nblk, K, BS), BF16),
            pltpu.VMEM((ITERS, 2 * ng, K, BS), BF16),
            pltpu.VMEM((RB, K, BS), BF16),
            pltpu.VMEM(tiles.shape, BF16),
            pltpu.VMEM((slots, K, BS), F32),
            pltpu.VMEM((3 * K, width), BF16),
            pltpu.VMEM((3 * K, width), BF16),
            pltpu.VMEM((8, 128), I32),
            pltpu.VMEM((8, 128), I32),
            pltpu.SMEM((8, 128), I32),
            pltpu.SMEM((128,), I32),
            pltpu.VMEM((8, 128), I32),
            pltpu.VMEM((2, nz, 8, 128), I32),
            pltpu.VMEM((2 * nz, 128), I32),
            pltpu.SMEM((2 * nz, 128), I32),
            pltpu.VMEM((calls, 96, 128), F32),
            pltpu.VMEM((calls, 2 * ng, prow, 128), F32),
            pltpu.VMEM((calls, nz, prow, 128), F32),
            pltpu.VMEM((calls, 96, 128), F32),
            pltpu.VMEM((K, 2 * K), F32),
            dma((3,)),
            dma((ITERS, 2, hops, NCH)),
            dma((ITERS, 2, hops, NCH)),
            dma((ITERS, 2, hops + 1, NCH)),
            dma((ITERS, 2, hops + 1, NCH)),
            dma((ITERS, ng)),
            dma((ITERS, ng)),
            dma((nz,)),
            dma((nz,)),
            dma((1,)),
            dma((1,)),
            dma((calls, pieces)),
            dma((calls, 2 * ng)),
            dma((calls, nz)),
            dma((calls, nz)),
            dma((calls, 2 * ng)),
            dma((calls, pieces)),
        ],
        compiler_params=pltpu.CompilerParams(
            collective_id=0, has_side_effects=True, vmem_limit_bytes=48 * 1024 * 1024
        ),
    )(
        sv, sd, tiles, jnp.stack([tile_row, tile_slot]), tile_count,
        send_row.reshape(1, -1), send_grp, ritz,
    )


def solution(mesh):
    spread = P(None, ("grp", "row"))
    flat = P(("grp", "row"))
    return jax.shard_map(
        functools.partial(shards, mesh.shape["grp"], mesh.shape["row"]),
        mesh=mesh,
        in_specs=(spread, spread, P(("grp", "row"), None, None)) + (flat,) * 5 + (P(),),
        out_specs=(spread, spread),
        check_vma=False,
    )
```

time: 1270 us -> 174 us (0.14); the launches traced: 1260 us -> 174 us
  waiting for transfers between devices: 1000 us -> 0 us
  Pallas kernels: 0 us -> 164 us
  other arithmetic: 135 us -> 0.68 us
  starting transfers between devices: 40.4 us -> 0 us
  matrix products: 33 us -> 0 us
  local copies, waits for them, and re-layouts: 28.9 us -> 7.5 us
  between operations: 17.9 us -> 1.29 us
    psum x2 -> x0, waiting for transfers between devices: 886 us -> none  [shards(): lax.psum(jnp.dot(stacked, stacked.T, precision=lax.Precision.HIGHEST), ('...]
    pallas_call x0 -> x1, Pallas kernels: none -> 164 us  [shards(): pl.pallas_call(functools.partial(kernel, ng, nz, width * ng * nr, slots),...]
    all_to_all x4 -> x0, waiting for transfers between devices: 114 us -> none  [the longest x2 105 us: shards(): lax.all_to_all(select_blocks(own_blocks, send_row), 'row', split_axis=1,...]
    another operation x24 -> x1, other arithmetic: 108 us -> 0.68 us  [shards(): jnp.stack([tile_row, tile_slot])]
    all_to_all x4 -> x0, starting transfers between devices: 40.1 us -> none  [the longest x2 27.3 us: shards(): lax.all_to_all(select_blocks(own_blocks, send_row), 'row', split_axis=1,...]
    dot_general x8 -> x0, matrix products: 21.8 us -> none  [the longest x2 7.74 us: shards(): lax.dot_general(picked, tiles, (((2,), (2,)), ((1,), (0,))), preferred_el...]
    gather x6 -> x0, local copies, waits for them, and re-layouts: 13.3 us -> none  [the longest x2 6.93 us: shards(): picked = jnp.take(block_table, tile_slot, axis=1)]
  transfers between devices with their start and end apart: 6 -> 0, of which waited for: 6 -> 0; matrix products, arithmetic and copies ran while one was open for 1% -> 0% of each run, Pallas kernels for 0% -> 0%
where the time goes in v1:
time: 174 us
  Pallas kernels  164 us (94%)
  local copies, waits for them, and re-layouts  7.5 us (4%)
    pallas_call x1, Pallas kernels, shards(): pl.pallas_call(functools.partial(kernel, ng, nz, width * ng * nr, slots),...  164 us
    unnamed x14, local copies, waits for them, and re-layouts  7.5 us

profile of v1, /device:TPU:1, one launch (start us, length us, event | category | flops | bytes accessed | tf_op | source)
XLA Modules:
  0.0 173.7 jit_solution(3681561734329363692)
XLA Ops:
  1.3 0.7 pad_add_fusion.meta
  2.0 0.0 copy-start
  2.0 2.0 %copy-done = bf16[104,128,128]{2,1,0:T(8,128)(2,1)S(1)} copy-done((bf16[104,128,128]{2,1,0:T(8,128)(2,1)S(1)}, bf16[104,128,128]{2,1,0:T(8,128)(2,1)}, u32[]{:S(2)}) %copy-start) | copy-done | bytes 3407896
  3.9 0.0 copy-start.1
  3.9 0.9 copy-done.1
  4.9 0.0 copy-start.2
  4.9 0.9 copy-done.2
  5.8 0.0 copy-start.3
  5.8 0.9 copy-done.3
  6.8 0.0 copy-start.4
  6.8 0.7 copy-done.4
  7.4 0.0 copy-start.5
  7.4 0.7 copy-done.5
  8.1 164.3 %shard_map.104 = (f32[64,1024]{1,0:T(8,128)S(1)}, f32[64,1024]{1,0:T(8,128)S(1)}) custom-call(f32[64,1024]{1,0:T(8,128)S(1)} %copy-done.1, f32[64,1024]{1,0:T(8,128)S(1)} %copy-done.2, bf16[104,128,128]{2,1,0:T(8,128)(2,1)S(1)} %copy-done, s32[2,104]{1,0:T(2,128)S(1)} %pad_add_fusion.meta, s32[1]{0:T(128)S(6)} %copy.13.count, s32[1,64]{1,0:T(1,128)S(1)} %bitcast.3, ...), custom_call_target="tpu_custom_call" | custom-call | tf_op jit(solution)/shard_map/pallas_call | solution.py:513
  172.3 0.7 copy.14
  173.0 0.7 copy.15
Async XLA Ops:
  2.0 2.0 %copy-start = (bf16[104,128,128]{2,1,0:T(8,128)(2,1)S(1)}, bf16[104,128,128]{2,1,0:T(8,128)(2,1)}, u32[]{:S(2)}) copy-start(bf16[104,128,128]{2,1,0:T(8,128)(2,1)} %tiles.1) | copy-start | bytes 10223620
  3.9 0.9 copy-start.1
  4.9 0.9 copy-start.2
  5.8 0.9 copy-start.3
  6.8 0.7 copy-start.4
  7.4 0.7 copy-start.5

commit v2 on v0

v2 whole, which is shorter than its diff:
```python
import functools

import jax
import jax.numpy as jnp
from jax import lax
from jax.experimental import pallas as pl
from jax.experimental.pallas import tpu as pltpu
from jax.sharding import PartitionSpec as P

ITERS = 2
K = 64
BS = 128
RB = 8
NCH = 4
BPC = RB // NCH
F32, BF16, I32 = jnp.float32, jnp.bfloat16, jnp.int32
MESH = pl.DeviceIdType.MESH
HIGH = lax.Precision.HIGHEST


def dot32(a, b, ca, cb):
    return lax.dot_general(
        a, b, (((ca,), (cb,)), ((), ())), precision=HIGH, preferred_element_type=F32
    )


def dot16(a, b, ca, cb):
    return lax.dot_general(a, b, (((ca,), (cb,)), ((), ())), preferred_element_type=F32)


def split(x):
    hi = x.astype(BF16)
    return hi, (x - hi.astype(F32)).astype(BF16)


def dot3(ah, al, bh, bl, ca, cb):
    return dot16(ah, bh, ca, cb) + (dot16(ah, bl, ca, cb) + dot16(al, bh, ca, cb))


class Eliminate:
    def __init__(self, s, work):
        row = lax.broadcasted_iota(I32, (K, K), 0)
        col = lax.broadcasted_iota(I32, (K, K), 1)
        work[:, 0:K] = s
        work[:, K : 2 * K] = jnp.where(row == col, 1.0, 0.0).astype(F32)
        self.rows = [work[8 * i : 8 * i + 8, :] for i in range(K // 8)]
        self.sub = lax.broadcasted_iota(I32, (8, 2 * K), 0)

    def panel(self, p):
        rows, sub = self.rows, self.sub
        wide = (8, 2 * K)
        cols = [
            [
                jnp.broadcast_to(rows[i][:, 8 * p + k : 8 * p + k + 1], wide)
                for i in range(p, K // 8)
            ]
            for k in range(8)
        ]
        for k in range(8):
            inv = lax.rsqrt(jnp.broadcast_to(cols[k][0][k : k + 1, :], wide))
            low = [c * inv for c in cols[k]]
            for j in range(k + 1, 8):
                mult = jnp.broadcast_to(low[0][j : j + 1, :], wide)
                cols[j] = [c - x * mult for c, x in zip(cols[j], low)]
            pivot = jnp.broadcast_to(rows[p][k : k + 1, :], wide) * inv
            below = jnp.where(sub > k, low[0], 0.0)
            rows[p] = jnp.where(sub == k, pivot, rows[p] - below * pivot)
            for i in range(p + 1, K // 8):
                rows[i] = rows[i] - low[i - p] * pivot

    def inverse(self):
        return jnp.concatenate([r[:, K : 2 * K] for r in self.rows], axis=0)


def eliminate(s, work):
    elim = Eliminate(s, work)
    for p in range(K // 8):
        elim.panel(p)
    return elim.inverse()


def tree_sum(xs):
    while len(xs) > 1:
        xs = [a + b for a, b in zip(xs[0::2], xs[1::2])] + ([xs[-1]] if len(xs) % 2 else [])
    return xs[0]


def near_positions(nz):
    return 2 * (nz // 2 * 5 // 8) + 1


def kernel(
    ng, nz, total_rows, slots,
    sv, sd, tiles, tile_row, tile_slot, count, send_row, send_grp, ritz,
    out_v, out_d,
    blk_a, blk_b, pack, own, tl, runs_a, runs_b, sh, sl, fd, rz, row_in, slot_in, row_list, iv, ov, sm_iv, sm_ix, sm_far,
    mytb, tb, tv, sm_tv, pay, rsb, zb, res, work,
    loc_sem, ring_s, ring_r, sib_s, sib_r, far_s, far_r, tb_s, tb_r, tbx_s, tbx_r,
    rs_s, rs_r, z_s, z_r, ag_s, ag_r,
):
    hops, pos_a = nz // 2, near_positions(nz)
    far0 = pos_a * 2 * RB
    rows_a, rows_b = far0 + 2 * ng, (nz - pos_a) * 2 * RB
    len_a, len_b = runs_a.shape[0], runs_b.shape[0]
    pieces = 12 if ng >= 12 else 3
    prow = 96 // pieces
    side = round(ng**0.5)
    g, r = lax.axis_index("grp"), lax.axis_index("row")
    z, c = r // 2, r % 2
    gx, gy = g // side, g % side
    m = g * 2 + c
    sib = (g, z * 2 + (1 - c))

    def remote(src, dst, ss, rs, dev):
        return pltpu.make_async_remote_copy(
            src_ref=src, dst_ref=dst, send_sem=ss, recv_sem=rs, device_id=dev, device_id_type=MESH
        )

    def wrap(i, n):
        return jnp.where(i >= n, i - n, i)

    z_steps = sorted(range(1, nz), key=lambda k: -min(k, nz - k))
    plane_steps = sorted(
        [(i, j, k) for i in range(side) for j in range(side) for k in range(2) if (i, j, k) != (0, 0, 0)],
        key=lambda t: -min(t[0], side - t[0]) - min(t[1], side - t[1]),
    )

    def z_dev(k):
        return (g, wrap(z + k, nz) * 2 + c)

    def plane_dev(t):
        core = 1 - c if t[2] else c
        return (wrap(gx + t[0], side) * side + wrap(gy + t[1], side), z * 2 + core)

    loads = [
        pltpu.make_async_copy(src, dst, loc_sem.at[i])
        for i, (src, dst) in enumerate(
            [(sv, out_v), (sd, fd), (tiles, tl), (tile_row, row_in), (tile_slot, slot_in),
             (send_row, row_list), (send_grp, sm_far), (ritz, rz)]
        )
    ]
    for cp in loads:
        cp.start()

    barrier = pltpu.get_barrier_semaphore()
    for k in z_steps:
        pl.semaphore_signal(barrier, inc=1, device_id=z_dev(k), device_id_type=MESH)
    for t in plane_steps:
        pl.semaphore_signal(barrier, inc=1, device_id=plane_dev(t), device_id_type=MESH)

    def place(d, hop):
        if hop == 0:
            return 0
        return nz - 1 if hop == hops else 2 * hop - 1 + d

    def chunk(it, pos, core, j=0, n=RB):
        if pos < pos_a:
            return blk_a.at[it, pl.ds(pos * 2 * RB + core * RB + j * BPC, n)]
        return blk_b.at[it, pl.ds((pos - pos_a) * 2 * RB + core * RB + j * BPC, n)]

    def ring_copy(it, d, hop, j):
        to = z_dev(1) if d == 0 else z_dev(nz - 1)
        return remote(
            chunk(it, place(d, hop - 1), c, j, BPC), chunk(it, place(d, hop), c, j, BPC),
            ring_s.at[it, d], ring_r.at[it, d, hop - 1, j], to,
        )

    def ring_here(it, d, hop, j):
        ref = chunk(it, place(d, hop), c, j, BPC)
        return remote(ref, ref, ring_s.at[it, d], ring_r.at[it, d, hop - 1, j], sib)

    def sib_copy(it, d, hop):
        pos = place(d, hop)
        half = hop == hops
        ref = chunk(it, pos, c, NCH // 2 if half and d else 0, RB // 2 if half else RB)
        return remote(ref, ref, sib_s.at[it], sib_r.at[it, int(pos >= pos_a)], sib)

    def ring_has(d, hop, j):
        return hop < hops or (hop == hops and (j < NCH // 2) == (d == 0))

    def far_copy(it, t):
        dev = plane_dev(t)
        return remote(
            pack.at[it, pl.ds(dev[0] * 2, 2)], blk_a.at[it, pl.ds(far0 + 2 * g, 2)],
            far_s.at[it], far_r.at[it], dev,
        )

    far_steps = [t for t in plane_steps if t[2] == 0]

    def drain_exchange(it):
        a, n = blk_a.at[it, pl.ds(0, nz * RB)], (hops - 1) * RB + RB // 2
        remote(a, a, sib_s.at[it], sib_r.at[it, 0], sib).wait_send()
        part = blk_a.at[it, pl.ds(0, n)]
        for d in range(2):
            remote(part, part, ring_s.at[it, d], ring_r.at[it, d, 0, 0], sib).wait_send()
        part = pack.at[it, pl.ds(0, 2 * ng - 2)]
        remote(part, part, far_s.at[it], far_r.at[it], sib).wait_send()

    owner = (g < pieces) & (c == lax.rem(g, 2))
    mine = pl.ds(pl.multiple_of(lax.rem(g, pieces) * prow, 8), prow)

    def is_mine(j):
        return (g == j) & (c == j % 2)

    def either(yes, no):
        @pl.when(owner)
        def _():
            yes()

        @pl.when(jnp.logical_not(owner))
        def _():
            no()

    def sum_start(k):
        for j in range(pieces):
            ref = pay.at[k, j * prow : (j + 1) * prow]

            @pl.when(is_mine(j))
            def _():
                rsb[k, m] = ref[...]

            @pl.when(jnp.logical_not(is_mine(j)))
            def _():
                remote(ref, rsb.at[k, m], rs_s.at[k], rs_r.at[k], (j, z * 2 + j % 2)).start()

    def sum_plane(k):
        @pl.when(owner)
        def _():
            ref = rsb.at[k, 0 : 2 * ng - 1]
            remote(ref, ref, rs_s.at[k], rs_r.at[k], sib).wait_recv()
            zb[k, z] = tree_sum([rsb[k, i] for i in range(2 * ng)])
            for s in z_steps:
                remote(zb.at[k, z], zb.at[k, z], z_s.at[k], z_r.at[k], z_dev(s)).start()

    def sum_z(k):
        @pl.when(owner)
        def _():
            ref = zb.at[k, 0 : nz - 1]
            remote(ref, ref, z_s.at[k], z_r.at[k], sib).wait_recv()
            res[k, mine] = tree_sum([zb[k, i] for i in range(nz)])
            for t in plane_steps:
                remote(res.at[k, mine], res.at[k, mine], ag_s.at[k], ag_r.at[k], plane_dev(t)).start()

    def sum_end(k):
        def wait(n):
            ref = res.at[k, 0 : n * prow]
            remote(ref, ref, ag_s.at[k], ag_r.at[k], sib).wait_recv()

        either(lambda: wait(pieces - 1), lambda: wait(pieces))

    def sum_drain(k):
        def wait(ref, sem):
            remote(ref, ref, sem, ag_r.at[k], sib).wait_send()

        def yes():
            wait(pay.at[k, 0 : (pieces - 1) * prow], rs_s.at[k])
            wait(zb.at[k, 0 : nz - 1], z_s.at[k])
            wait(rsb.at[k, 0 : 2 * ng - 1], ag_s.at[k])

        either(yes, lambda: wait(pay.at[k], rs_s.at[k]))

    def put_sums(k, wide, square):
        pay[k, 0:K, :] = wide
        pay[k, K : K + K // 2, 0:K] = square[0 : K // 2]
        pay[k, K : K + K // 2, K : 2 * K] = square[K // 2 : K]

    def get_sums(k):
        scale = 1.0 / total_rows
        left = res[k, 0:K, 0:K] * scale
        right = res[k, 0:K, K : 2 * K] * scale
        square = jnp.concatenate(
            [res[k, K : K + K // 2, 0:K], res[k, K : K + K // 2, K : 2 * K]], axis=0
        )
        return left, right, square * scale

    def order_tiles():
        loads[3].wait()
        loads[4].wait()
        iv[...] = jnp.zeros((8, 128), I32)
        iv[0:1, 0:slots] = row_in[...]
        iv[1:2, 0:slots] = slot_in[...]
        lane = lax.broadcasted_iota(I32, (128, 128), 1)
        subl = lax.broadcasted_iota(I32, (128, 128), 0)
        row_r = jnp.broadcast_to(iv[0:1, :], (128, 128))
        slot_r = jnp.broadcast_to(iv[1:2, :], (128, 128))
        step = lax.shift_right_arithmetic(slot_r - RB, 2) - z
        step = jnp.where(step < 0, step + nz, step)
        late = (slot_r >= RB) & (slot_r < RB + 4 * nz)
        late = late & (jnp.minimum(step, nz - step) * 2 >= pos_a)
        key_r = jnp.where(late, 1024, 0) + row_r * 128 + lane
        key_r = jnp.where(lane < count[0], key_r, 4096 + lane)
        row_c, slot_c, key_c = row_r.T, slot_r.T, key_r.T
        rank_r = jnp.sum(jnp.where(key_c < key_r, 1, 0), axis=0, keepdims=True)
        hit = jnp.broadcast_to(rank_r, (128, 128)).T == lane

        def total(x):
            return jnp.sum(x, axis=0, keepdims=True)

        ov[...] = jnp.zeros((8, 128), I32)
        ov[0:1, :] = total(jnp.where(hit, subl, 0))
        ov[1:2, :] = total(jnp.where(hit, slot_c, 0))
        ov[2:3, :] = total(jnp.where(hit, row_c, 0))
        ov[3:4, :] = total(jnp.where((key_c < 1024) & (row_c <= lane), 1, 0))
        ov[4:5, :] = total(jnp.where((key_c >= 1024) & (key_c < 4096) & (row_c <= lane), 1, 0))
        pltpu.make_async_copy(ov, sm_iv, loc_sem.at[8]).start()

    def send_table():
        loads[5].wait()
        mytb[...] = jnp.zeros((8, 128), I32)
        mytb[0:1, 0 : 4 * nz] = row_list[...]
        tb[c, z] = mytb[...]
        for k in z_steps:
            remote(mytb, tb.at[c, z], tb_s.at[0], tb_r.at[0], z_dev(k)).start()

    def pass_table():
        ref = tb.at[0, 0 : nz - 1]
        remote(ref, ref, tb_s.at[0], tb_r.at[0], sib).wait_recv()
        remote(tb.at[c], tb.at[c], tbx_s.at[0], tbx_r.at[0], sib).start()

    def take_table():
        remote(tb.at[1 - c], tb.at[1 - c], tbx_s.at[0], tbx_r.at[0], sib).wait_recv()
        for i in range(2 * nz):
            tv[i : i + 1, :] = tb[i % 2, i // 2, 0:1, :]
        pltpu.make_async_copy(tv, sm_tv, loc_sem.at[9]).start()

    def read_table():
        pltpu.make_async_copy(ov, sm_iv, loc_sem.at[8]).wait()
        pltpu.make_async_copy(tv, sm_tv, loc_sem.at[9]).wait()

    def index_tiles(first, last):
        def step(i, carry):
            e = jnp.clip(sm_iv[1, i], 0, RB + 4 * nz + 2 * ng - 1)
            p = jnp.clip(lax.shift_right_arithmetic(e - RB, 1), 0, 2 * nz - 1)
            q = jnp.clip(sm_tv[p, 2 * r + (e & 1)], 0, RB - 1)
            away = lax.shift_right_arithmetic(p, 1) - z
            away = jnp.where(away < 0, away + nz, away)
            pos = jnp.where(away < hops, 2 * away, 2 * (nz - away) - 1)
            pos = jnp.where(pos >= pos_a, pos - pos_a, pos)
            near = pos * 2 * RB + (p & 1) * RB + q
            far = far0 + jnp.clip(e - RB - 4 * nz, 0, 2 * ng - 1)
            sm_ix[i] = jnp.where(e < RB, c * RB + e, jnp.where(e < RB + 4 * nz, near, far))
            return carry

        lax.fori_loop(first, last, step, 0)

    def tile_step(acc, block, i, fresh):
        product = dot16(block, tl[jnp.clip(sm_iv[0, i], 0, slots - 1)], 1, 1)
        if fresh:
            return product
        keep = jnp.where(sm_iv[2, i] == sm_iv[2, i - 1], 1.0, 0.0).astype(F32)
        return acc * keep + product

    def tiles_early(it, state, first, last):
        acc = state.get("acc")
        for i in range(first, min(last, len_a)):
            acc = tile_step(acc, blk_a[it, jnp.clip(sm_ix[i], 0, rows_a - 1)], i, i == 0)
            runs_a[i] = acc
        state["acc"] = acc

    def tiles_late(it):
        first, acc = jnp.clip(sm_iv[3, RB - 1], 0, len_a), None
        for u in range(len_b):
            i = first + u
            acc = tile_step(acc, blk_b[it, jnp.clip(sm_ix[i], 0, rows_b - 1)], i, u == 0)
            runs_b[u] = acc
        for b in range(RB):
            x = 0.0
            for line, runs, size in ((3, runs_a, len_a), (4, runs_b, len_b)):
                end = sm_iv[line, b]
                before = sm_iv[line, b - 1] if b else jnp.int32(0)
                some = jnp.where(end > before, 1.0, 0.0).astype(F32)
                x = x + runs[jnp.clip(end - 1, 0, size - 1)] * some
            hi, lo = split(x)
            sh[2 * K : 3 * K, b * BS : (b + 1) * BS] = hi
            sl[2 * K : 3 * K, b * BS : (b + 1) * BS] = lo

    def split_into(row0, x):
        hi, lo = split(x)
        sh[row0 : row0 + K, :] = hi
        sl[row0 : row0 + K, :] = lo

    def put_vectors(it, x):
        split_into(0, x)
        for b in range(RB):
            part = sh[0:K, b * BS : (b + 1) * BS]
            own[b] = part
            blk_a[it, c * RB + b] = part

    def send_far(it):
        if it == 0:
            loads[6].wait()
        for h in range(ng):
            for s in range(2):
                pack[it, h * 2 + s] = own[jnp.clip(sm_far[h * 2 + s], 0, RB - 1)]
        zero = jnp.zeros((K, BS), BF16)
        blk_a[it, far0 + 2 * g] = zero
        blk_a[it, far0 + 2 * g + 1] = zero
        for t in far_steps:
            far_copy(it, t).start()

    def wait_early(it):
        ref = blk_a.at[it, pl.ds(0, pos_a * RB)]
        remote(ref, ref, sib_s.at[it], sib_r.at[it, 0], sib).wait_recv()
        ref = blk_a.at[it, pl.ds(0, 2 * ng - 2)]
        remote(ref, ref, far_s.at[it], far_r.at[it], sib).wait_recv()

    def wait_late(it):
        ref = blk_b.at[it, pl.ds(0, (nz - pos_a) * RB)]
        remote(ref, ref, sib_s.at[it], sib_r.at[it, 1], sib).wait_recv()

    def first_products():
        put_sums(
            0,
            dot3(sh[0:K], sl[0:K], sh[0 : 2 * K], sl[0 : 2 * K], 1, 1),
            dot3(sh[K : 2 * K], sl[K : 2 * K], sh[K : 2 * K], sl[K : 2 * K], 1, 1),
        )

    def get_directions(it):
        if it == 0:
            loads[1].wait()
        split_into(K, fd[...])

    loads[0].wait()
    put_vectors(0, out_v[...])
    pl.semaphore_wait(barrier, nz - 1 + 2 * ng - 1)

    for it in range(ITERS):
        k0, k1 = 0, 1 + it
        for j in range(NCH):
            for d in range(2):
                ring_copy(it, d, 1, j).start()
        sib_copy(it, 0, 0).start()

        state = {}
        early = hops * 5 // 8 * NCH + 1
        ready = early - max(1, NCH // 2)
        last = (hops - 1) * NCH + NCH // 2
        plan = [(0, functools.partial(send_far, it)), (1, functools.partial(get_directions, it))]
        if it == 0:
            mid = ready // 2 + 1
            tail = max(mid + 2, ready - 4)
            plan += [
                (0, send_table),
                (2, first_products),
                (2, functools.partial(sum_start, k0)),
                (3, order_tiles),
                (mid, functools.partial(sum_plane, k0)),
                (mid + 1, pass_table),
                (tail, take_table),
                (tail + 1, read_table),
                (max(mid + 2, last - 4), functools.partial(sum_z, k0)),
            ]
            part = -(-slots // 3)
            for i in range(3):
                plan += [(tail + 1 + i, functools.partial(index_tiles, i * part, min(slots, (i + 1) * part)))]
            early = max(early, tail + 4)
        plan += [(early, functools.partial(wait_early, it))]
        if it == 0:
            plan += [(early, lambda: loads[2].wait())]
        part = -(-len_a // max(1, last - early))
        for i in range(-(-len_a // part)):
            plan += [(early + i, functools.partial(tiles_early, it, state, i * part, (i + 1) * part))]
        plan = sorted(enumerate(plan), key=lambda t: (t[1][0], t[0]))
        plan = [t[1] for t in plan]

        step = 0
        for hop in range(1, hops + 1):
            for j in range(NCH):
                for d in range(2):
                    if ring_has(d, hop, j):
                        ring_here(it, d, hop, j).wait_recv()
                        if ring_has(d, hop + 1, j):
                            ring_copy(it, d, hop + 1, j).start()
                        if not ring_has(d, hop, j + 1) or j == NCH - 1:
                            sib_copy(it, d, hop).start()
                while plan and plan[0][0] <= step:
                    plan.pop(0)[1]()
                step += 1
        for _, work_left in plan:
            work_left()
        wait_late(it)
        tiles_late(it)
        put_sums(
            k1,
            dot3(sh[2 * K : 3 * K], sl[2 * K : 3 * K], sh[0 : 2 * K], sl[0 : 2 * K], 1, 1),
            dot3(sh[2 * K : 3 * K], sl[2 * K : 3 * K], sh[2 * K : 3 * K], sl[2 * K : 3 * K], 1, 1),
        )
        sum_start(k1)
        if it == 0:
            sum_end(k0)
            g_vv, g_vd, g_dd = get_sums(k0)
            loads[7].wait()
        else:
            before = rz[it - 1]
            wide = dot32(before, before, 0, 0)
            g_vv, g_vd, g_dd = wide[0:K, 0:K], wide[0:K, K : 2 * K], wide[K : 2 * K, K : 2 * K]
        e_v = eliminate(g_vv, work)
        u_d = dot32(e_v, g_vd, 1, 0)
        s_dd = g_dd - dot32(u_d, u_d, 0, 0)
        sum_plane(k1)
        d_e = dot32(u_d, e_v, 0, 0)
        sum_z(k1)
        sum_end(k1)
        g_av, g_ad, g_aa = get_sums(k1)
        u_a = dot32(e_v, g_av, 1, 1)
        s_aa = g_aa - dot32(u_a, u_a, 0, 0)
        s_ad = g_ad - dot32(u_a, u_d, 0, 0)
        e_a = eliminate(s_aa, work)
        u_ad = dot32(e_a, s_ad, 1, 0)
        e_d = eliminate(s_dd - dot32(u_ad, u_ad, 0, 0), work)
        a_v = -dot32(e_a, dot32(u_a, e_v, 0, 0), 1, 0)
        d_v = -dot32(e_d, d_e + dot32(u_ad, a_v, 0, 0), 1, 0)
        d_a = -dot32(e_d, dot32(u_ad, e_a, 0, 0), 1, 0)
        rz_v, rz_a, rz_d = (rz[it, i * K : (i + 1) * K, :] for i in range(3))
        c_v = dot32(rz_v, e_v, 0, 0) + dot32(rz_a, a_v, 0, 0) + dot32(rz_d, d_v, 0, 0)
        c_a = dot32(rz_a, e_a, 0, 0) + dot32(rz_d, d_a, 0, 0)
        c_d = dot32(rz_d, e_d, 0, 0)
        ch, cl = split(jnp.concatenate([c_v, c_d, c_a], axis=1))
        if it + 1 < ITERS:
            x = dot3(ch[0:K], cl[0:K], sh[...], sl[...], 1, 0)
            y = dot3(ch[K : 2 * K], cl[K : 2 * K], sh[...], sl[...], 1, 0)
            put_vectors(it + 1, x)
            fd[...] = y
        else:
            new = dot3(ch, cl, sh[...], sl[...], 1, 0)
            out_v[...] = new[0:K]
            out_d[...] = new[K : 2 * K]

    ref = tb.at[0, 0 : nz - 1]
    remote(ref, ref, tb_s.at[0], tb_r.at[0], sib).wait_send()
    remote(tb.at[c], tb.at[c], tbx_s.at[0], tbx_r.at[0], sib).wait_send()
    for it in range(ITERS):
        drain_exchange(it)
    for k in range(1 + ITERS):
        sum_drain(k)


def shards(ng, nr, sv, sd, tiles, tile_row, tile_slot, tile_count, send_row, send_grp, ritz):
    nz = nr // 2
    slots, width = tiles.shape[0], sv.shape[1]
    pos_a = near_positions(nz)
    far0 = pos_a * 2 * RB
    len_a = RB + 2 * (ng - 1) + 2 * (2 * pos_a - 1)
    len_b = 4 * (nz - pos_a)
    pieces = 12 if ng >= 12 else 3
    prow = 96 // pieces
    calls = 1 + ITERS
    dma = pltpu.SemaphoreType.DMA
    vmem, smem = pl.BlockSpec(memory_space=pltpu.VMEM), pl.BlockSpec(memory_space=pltpu.SMEM)
    hbm = pl.BlockSpec(memory_space=pl.ANY)
    return pl.pallas_call(
        functools.partial(kernel, ng, nz, width * ng * nr, slots),
        out_shape=[jax.ShapeDtypeStruct(sv.shape, F32)] * 2,
        in_specs=[hbm] * 5 + [smem] + [hbm] * 3,
        out_specs=[vmem, vmem],
        scratch_shapes=[
            pltpu.VMEM((ITERS, far0 + 2 * ng, K, BS), BF16),
            pltpu.VMEM((ITERS, (nz - pos_a) * 2 * RB, K, BS), BF16),
            pltpu.VMEM((ITERS, 2 * ng, K, BS), BF16),
            pltpu.VMEM((RB, K, BS), BF16),
            pltpu.VMEM(tiles.shape, BF16),
            pltpu.VMEM((len_a, K, BS), F32),
            pltpu.VMEM((len_b, K, BS), F32),
            pltpu.VMEM((3 * K, width), BF16),
            pltpu.VMEM((3 * K, width), BF16),
            pltpu.VMEM((K, width), F32),
            pltpu.VMEM(ritz.shape, F32),
            pltpu.VMEM((1, slots), I32),
            pltpu.VMEM((1, slots), I32),
            pltpu.VMEM((1, 4 * nz), I32),
            pltpu.VMEM((8, 128), I32),
            pltpu.VMEM((8, 128), I32),
            pltpu.SMEM((8, 128), I32),
            pltpu.SMEM((128,), I32),
            pltpu.SMEM(send_grp.shape, I32),
            pltpu.VMEM((8, 128), I32),
            pltpu.VMEM((2, nz, 8, 128), I32),
            pltpu.VMEM((2 * nz, 128), I32),
            pltpu.SMEM((2 * nz, 128), I32),
            pltpu.VMEM((calls, 96, 128), F32),
            pltpu.VMEM((calls, 2 * ng, prow, 128), F32),
            pltpu.VMEM((calls, nz, prow, 128), F32),
            pltpu.VMEM((calls, 96, 128), F32),
            pltpu.VMEM((K, 2 * K), F32),
            dma((10,)),
            dma((ITERS, 2)),
            dma((ITERS, 2, nz // 2, NCH)),
            dma((ITERS,)),
            dma((ITERS, 2)),
            dma((ITERS,)),
            dma((ITERS,)),
            dma((1,)),
            dma((1,)),
            dma((1,)),
            dma((1,)),
            dma((calls,)),
            dma((calls,)),
            dma((calls,)),
            dma((calls,)),
            dma((calls,)),
            dma((calls,)),
        ],
        compiler_params=pltpu.CompilerParams(
            collective_id=0, has_side_effects=True, vmem_limit_bytes=60 * 1024 * 1024
        ),
    )(
        sv, sd, tiles, tile_row.reshape(1, -1), tile_slot.reshape(1, -1), tile_count,
        send_row.reshape(1, -1), send_grp, ritz,
    )


def solution(mesh):
    spread = P(None, ("grp", "row"))
    flat = P(("grp", "row"))
    return jax.shard_map(
        functools.partial(shards, mesh.shape["grp"], mesh.shape["row"]),
        mesh=mesh,
        in_specs=(spread, spread, P(("grp", "row"), None, None)) + (flat,) * 5 + (P(),),
        out_specs=(spread, spread),
        check_vma=False,
    )
```

time: 1270 us -> 134 us (0.11); the launches traced: 1260 us -> 134 us
  waiting for transfers between devices: 1000 us -> 0 us
  other arithmetic: 135 us -> 0 us
  Pallas kernels: 0 us -> 130 us
  starting transfers between devices: 40.4 us -> 0 us
  matrix products: 33 us -> 0 us
  local copies, waits for them, and re-layouts: 28.9 us -> 3.34 us
  between operations: 17.9 us -> 1.29 us
    psum x2 -> x0, waiting for transfers between devices: 886 us -> none  [shards(): lax.psum(jnp.dot(stacked, stacked.T, precision=lax.Precision.HIGHEST), ('...]
    pallas_call x0 -> x1, Pallas kernels: none -> 130 us  [shards(): pl.pallas_call(functools.partial(kernel, ng, nz, width * ng * nr, slots),...]
    all_to_all x4 -> x0, waiting for transfers between devices: 114 us -> none  [the longest x2 105 us: shards(): lax.all_to_all(select_blocks(own_blocks, send_row), 'row', split_axis=1,...]
    another operation x24 -> x0, other arithmetic: 108 us -> none  [the longest x14 63.9 us: shards(): factor = jnp.linalg.cholesky(gram_matrix)]
    all_to_all x4 -> x0, starting transfers between devices: 40.1 us -> none  [the longest x2 27.3 us: shards(): lax.all_to_all(select_blocks(own_blocks, send_row), 'row', split_axis=1,...]
    dot_general x8 -> x0, matrix products: 21.8 us -> none  [the longest x2 7.74 us: shards(): lax.dot_general(picked, tiles, (((2,), (2,)), ((1,), (0,))), preferred_el...]
    gather x6 -> x0, local copies, waits for them, and re-layouts: 13.3 us -> none  [the longest x2 6.93 us: shards(): picked = jnp.take(block_table, tile_slot, axis=1)]
  transfers between devices with their start and end apart: 6 -> 0, of which waited for: 6 -> 0; matrix products, arithmetic and copies ran while one was open for 1% -> 0% of each run, Pallas kernels for 0% -> 0%
where the time goes in v2:
time: 134 us
  Pallas kernels  130 us (97%)
  local copies, waits for them, and re-layouts  3.34 us (2%)
    pallas_call x1, Pallas kernels, shards(): pl.pallas_call(functools.partial(kernel, ng, nz, width * ng * nr, slots),...  130 us
    unnamed x2, local copies, waits for them, and re-layouts  3.34 us

profile of v2, /device:TPU:1, one launch (start us, length us, event | category | flops | bytes accessed | tf_op | source)
XLA Modules:
  0.0 134.3 jit_solution(12263708155833172911)
XLA Ops:
  1.3 129.7 %shard_map.104 = (f32[64,1024]{1,0:T(8,128)}, f32[64,1024]{1,0:T(8,128)}) custom-call(f32[64,1024]{1,0:T(8,128)} %sv.1, f32[64,1024]{1,0:T(8,128)} %sd.1, bf16[104,128,128]{2,1,0:T(8,128)(2,1)} %tiles.1, s32[1,104]{1,0:T(1,128)} %bitcast.3, s32[1,104]{1,0:T(1,128)} %bitcast.4, s32[1]{0:T(128)S(6)} %copy.13.count, s32[1,64]{1,0:T(1,128)} %bitcast.5, ...), custom_call_target="tpu_custom_call" | custom-call | tf_op jit(solution)/shard_map/pallas_call | solution.py:551
  131.0 1.7 %copy.14 = f32[64,1024]{1,0:T(8,128)} copy(f32[64,1024]{1,0:T(8,128)} %get-tuple-element.4) | data formatting | bytes 524288
  132.6 1.7 %copy.15 = f32[64,1024]{1,0:T(8,128)} copy(f32[64,1024]{1,0:T(8,128)} %get-tuple-element.5) | data formatting | bytes 524288

commit v3 on v2

--- a/solution.py
+++ b/solution.py
@@ -92,9 +92,9 @@
 def kernel(
     ng, nz, total_rows, slots,
     sv, sd, tiles, tile_row, tile_slot, count, send_row, send_grp, ritz,
-    out_v, out_d,
-    blk_a, blk_b, pack, own, tl, runs_a, runs_b, sh, sl, fd, rz, row_in, slot_in, row_list, iv, ov, sm_iv, sm_ix, sm_far,
-    mytb, tb, tv, sm_tv, pay, rsb, zb, res, work,
+    out,
+    blk_a, blk_b, pack, own, tl, runs_a, runs_b, sh, sl, fd, rz, row_in, slot_in, row_list, iv, ov, sm_iv, sm_count, sm_far,
+    mytb, tb, tv, pay, rsb, zb, res, work,
     loc_sem, ring_s, ring_r, sib_s, sib_r, far_s, far_r, tb_s, tb_r, tbx_s, tbx_r,
     rs_s, rs_r, z_s, z_r, ag_s, ag_r,
 ):
@@ -135,8 +135,8 @@
     loads = [
         pltpu.make_async_copy(src, dst, loc_sem.at[i])
         for i, (src, dst) in enumerate(
-            [(sv, out_v), (sd, fd), (tiles, tl), (tile_row, row_in), (tile_slot, slot_in),
-             (send_row, row_list), (send_grp, sm_far), (ritz, rz)]
+            [(sv, out.at[0:K]), (sd, fd), (tiles, tl), (tile_row, row_in), (tile_slot, slot_in),
+             (send_row, row_list), (send_grp, sm_far), (ritz, rz), (count, sm_count)]
         )
     ]
     for cp in loads:
@@ -196,18 +196,23 @@
         part = pack.at[it, pl.ds(0, 2 * ng - 2)]
         remote(part, part, far_s.at[it], far_r.at[it], sib).wait_send()
 
-    owner = (g < pieces) & (c == lax.rem(g, 2))
     mine = pl.ds(pl.multiple_of(lax.rem(g, pieces) * prow, 8), prow)
 
-    def is_mine(j):
-        return (g == j) & (c == j % 2)
-
-    def either(yes, no):
-        @pl.when(owner)
+    def owner_core(k, j):
+        return (j + (k == 0)) % 2
+
+    def owner(k):
+        return (g < pieces) & (c == lax.rem(g + (k == 0), 2))
+
+    def is_mine(k, j):
+        return (g == j) & (c == owner_core(k, j))
+
+    def either(k, yes, no):
+        @pl.when(owner(k))
         def _():
             yes()
 
-        @pl.when(jnp.logical_not(owner))
+        @pl.when(jnp.logical_not(owner(k)))
         def _():
             no()
 
@@ -215,16 +220,16 @@
         for j in range(pieces):
             ref = pay.at[k, j * prow : (j + 1) * prow]
 
-            @pl.when(is_mine(j))
+            @pl.when(is_mine(k, j))
             def _():
                 rsb[k, m] = ref[...]
 
-            @pl.when(jnp.logical_not(is_mine(j)))
+            @pl.when(jnp.logical_not(is_mine(k, j)))
             def _():
-                remote(ref, rsb.at[k, m], rs_s.at[k], rs_r.at[k], (j, z * 2 + j % 2)).start()
+                remote(ref, rsb.at[k, m], rs_s.at[k], rs_r.at[k], (j, z * 2 + owner_core(k, j))).start()
 
     def sum_plane(k):
-        @pl.when(owner)
+        @pl.when(owner(k))
         def _():
             ref = rsb.at[k, 0 : 2 * ng - 1]
             remote(ref, ref, rs_s.at[k], rs_r.at[k], sib).wait_recv()
@@ -233,7 +238,7 @@
                 remote(zb.at[k, z], zb.at[k, z], z_s.at[k], z_r.at[k], z_dev(s)).start()
 
     def sum_z(k):
-        @pl.when(owner)
+        @pl.when(owner(k))
         def _():
             ref = zb.at[k, 0 : nz - 1]
             remote(ref, ref, z_s.at[k], z_r.at[k], sib).wait_recv()
@@ -246,7 +251,7 @@
             ref = res.at[k, 0 : n * prow]
             remote(ref, ref, ag_s.at[k], ag_r.at[k], sib).wait_recv()
 
-        either(lambda: wait(pieces - 1), lambda: wait(pieces))
+        either(k, lambda: wait(pieces - 1), lambda: wait(pieces))
 
     def sum_drain(k):
         def wait(ref, sem):
@@ -257,7 +262,7 @@
             wait(zb.at[k, 0 : nz - 1], z_s.at[k])
             wait(rsb.at[k, 0 : 2 * ng - 1], ag_s.at[k])
 
-        either(yes, lambda: wait(pay.at[k], rs_s.at[k]))
+        either(k, yes, lambda: wait(pay.at[k], rs_s.at[k]))
 
     def put_sums(k, wide, square):
         pay[k, 0:K, :] = wide
@@ -274,8 +279,8 @@
         return left, right, square * scale
 
     def order_tiles():
-        loads[3].wait()
-        loads[4].wait()
+        for i in (3, 4, 8):
+            loads[i].wait()
         iv[...] = jnp.zeros((8, 128), I32)
         iv[0:1, 0:slots] = row_in[...]
         iv[1:2, 0:slots] = slot_in[...]
@@ -288,7 +293,7 @@
         late = (slot_r >= RB) & (slot_r < RB + 4 * nz)
         late = late & (jnp.minimum(step, nz - step) * 2 >= pos_a)
         key_r = jnp.where(late, 1024, 0) + row_r * 128 + lane
-        key_r = jnp.where(lane < count[0], key_r, 4096 + lane)
+        key_r = jnp.where(lane < sm_count[0], key_r, 4096 + lane)
         row_c, slot_c, key_c = row_r.T, slot_r.T, key_r.T
         rank_r = jnp.sum(jnp.where(key_c < key_r, 1, 0), axis=0, keepdims=True)
         hit = jnp.broadcast_to(rank_r, (128, 128)).T == lane
@@ -302,7 +307,6 @@
         ov[2:3, :] = total(jnp.where(hit, row_c, 0))
         ov[3:4, :] = total(jnp.where((key_c < 1024) & (row_c <= lane), 1, 0))
         ov[4:5, :] = total(jnp.where((key_c >= 1024) & (key_c < 4096) & (row_c <= lane), 1, 0))
-        pltpu.make_async_copy(ov, sm_iv, loc_sem.at[8]).start()
 
     def send_table():
         loads[5].wait()
@@ -319,29 +323,31 @@
 
     def take_table():
         remote(tb.at[1 - c], tb.at[1 - c], tbx_s.at[0], tbx_r.at[0], sib).wait_recv()
+        tv[...] = jnp.zeros((128, 128), I32)
         for i in range(2 * nz):
             tv[i : i + 1, :] = tb[i % 2, i // 2, 0:1, :]
-        pltpu.make_async_copy(tv, sm_tv, loc_sem.at[9]).start()
+        tv[...] = tv[...].T
+
+    def index_tiles():
+        def column(s):
+            return jnp.broadcast_to(tv[pl.ds(2 * r + s, 1), :], (128, 128)).T
+
+        sender = lax.broadcasted_iota(I32, (128, 128), 0)
+        e = ov[1:2, :]
+        p = lax.shift_right_arithmetic(e - RB, 1)
+        listed = jnp.where(jnp.broadcast_to(e & 1, (128, 128)) == 0, column(0), column(1))
+        q = jnp.sum(jnp.where(sender == jnp.broadcast_to(p, (128, 128)), listed, 0), axis=0, keepdims=True)
+        away = lax.shift_right_arithmetic(p, 1) - z
+        away = jnp.where(away < 0, away + nz, away)
+        pos = jnp.where(away < hops, 2 * away, 2 * (nz - away) - 1)
+        pos = jnp.where(pos >= pos_a, pos - pos_a, pos)
+        near = pos * 2 * RB + (p & 1) * RB + q
+        far = far0 + e - RB - 4 * nz
+        ov[5:6, :] = jnp.where(e < RB, c * RB + e, jnp.where(e < RB + 4 * nz, near, far))
+        pltpu.make_async_copy(ov, sm_iv, loc_sem.at[9]).start()
 
     def read_table():
-        pltpu.make_async_copy(ov, sm_iv, loc_sem.at[8]).wait()
-        pltpu.make_async_copy(tv, sm_tv, loc_sem.at[9]).wait()
-
-    def index_tiles(first, last):
-        def step(i, carry):
-            e = jnp.clip(sm_iv[1, i], 0, RB + 4 * nz + 2 * ng - 1)
-            p = jnp.clip(lax.shift_right_arithmetic(e - RB, 1), 0, 2 * nz - 1)
-            q = jnp.clip(sm_tv[p, 2 * r + (e & 1)], 0, RB - 1)
-            away = lax.shift_right_arithmetic(p, 1) - z
-            away = jnp.where(away < 0, away + nz, away)
-            pos = jnp.where(away < hops, 2 * away, 2 * (nz - away) - 1)
-            pos = jnp.where(pos >= pos_a, pos - pos_a, pos)
-            near = pos * 2 * RB + (p & 1) * RB + q
-            far = far0 + jnp.clip(e - RB - 4 * nz, 0, 2 * ng - 1)
-            sm_ix[i] = jnp.where(e < RB, c * RB + e, jnp.where(e < RB + 4 * nz, near, far))
-            return carry
-
-        lax.fori_loop(first, last, step, 0)
+        pltpu.make_async_copy(ov, sm_iv, loc_sem.at[9]).wait()
 
     def tile_step(acc, block, i, fresh):
         product = dot16(block, tl[jnp.clip(sm_iv[0, i], 0, slots - 1)], 1, 1)
@@ -353,7 +359,7 @@
     def tiles_early(it, state, first, last):
         acc = state.get("acc")
         for i in range(first, min(last, len_a)):
-            acc = tile_step(acc, blk_a[it, jnp.clip(sm_ix[i], 0, rows_a - 1)], i, i == 0)
+            acc = tile_step(acc, blk_a[it, jnp.clip(sm_iv[5, i], 0, rows_a - 1)], i, i == 0)
             runs_a[i] = acc
         state["acc"] = acc
 
@@ -361,7 +367,7 @@
         first, acc = jnp.clip(sm_iv[3, RB - 1], 0, len_a), None
         for u in range(len_b):
             i = first + u
-            acc = tile_step(acc, blk_b[it, jnp.clip(sm_ix[i], 0, rows_b - 1)], i, u == 0)
+            acc = tile_step(acc, blk_b[it, jnp.clip(sm_iv[5, i], 0, rows_b - 1)], i, u == 0)
             runs_b[u] = acc
         for b in range(RB):
             x = 0.0
@@ -421,7 +427,7 @@
         split_into(K, fd[...])
 
     loads[0].wait()
-    put_vectors(0, out_v[...])
+    put_vectors(0, out[0:K])
     pl.semaphore_wait(barrier, nz - 1 + 2 * ng - 1)
 
     for it in range(ITERS):
@@ -447,12 +453,9 @@
                 (mid, functools.partial(sum_plane, k0)),
                 (mid + 1, pass_table),
                 (tail, take_table),
-                (tail + 1, read_table),
-                (max(mid + 2, last - 4), functools.partial(sum_z, k0)),
+                (tail + 1, index_tiles),
+                (tail + 3, read_table),
             ]
-            part = -(-slots // 3)
-            for i in range(3):
-                plan += [(tail + 1 + i, functools.partial(index_tiles, i * part, min(slots, (i + 1) * part)))]
             early = max(early, tail + 4)
         plan += [(early, functools.partial(wait_early, it))]
         if it == 0:
@@ -487,18 +490,23 @@
         )
         sum_start(k1)
         if it == 0:
+            loads[7].wait()
+            sum_z(k0)
+            sum_plane(k1)
             sum_end(k0)
             g_vv, g_vd, g_dd = get_sums(k0)
-            loads[7].wait()
         else:
             before = rz[it - 1]
             wide = dot32(before, before, 0, 0)
             g_vv, g_vd, g_dd = wide[0:K, 0:K], wide[0:K, K : 2 * K], wide[K : 2 * K, K : 2 * K]
+        rz_v, rz_a, rz_d = (rz[it, i * K : (i + 1) * K, :] for i in range(3))
         e_v = eliminate(g_vv, work)
         u_d = dot32(e_v, g_vd, 1, 0)
         s_dd = g_dd - dot32(u_d, u_d, 0, 0)
-        sum_plane(k1)
+        if it:
+            sum_plane(k1)
         d_e = dot32(u_d, e_v, 0, 0)
+        v_e = dot32(rz_v, e_v, 0, 0)
         sum_z(k1)
         sum_end(k1)
         g_av, g_ad, g_aa = get_sums(k1)
@@ -507,14 +515,15 @@
         s_ad = g_ad - dot32(u_a, u_d, 0, 0)
         e_a = eliminate(s_aa, work)
         u_ad = dot32(e_a, s_ad, 1, 0)
+        a_v = -dot32(e_a, dot32(u_a, e_v, 0, 0), 1, 0)
+        d_v = d_e + dot32(u_ad, a_v, 0, 0)
+        d_a = dot32(u_ad, e_a, 0, 0)
+        c_v = v_e + dot32(rz_a, a_v, 0, 0)
+        c_a = dot32(rz_a, e_a, 0, 0)
         e_d = eliminate(s_dd - dot32(u_ad, u_ad, 0, 0), work)
-        a_v = -dot32(e_a, dot32(u_a, e_v, 0, 0), 1, 0)
-        d_v = -dot32(e_d, d_e + dot32(u_ad, a_v, 0, 0), 1, 0)
-        d_a = -dot32(e_d, dot32(u_ad, e_a, 0, 0), 1, 0)
-        rz_v, rz_a, rz_d = (rz[it, i * K : (i + 1) * K, :] for i in range(3))
-        c_v = dot32(rz_v, e_v, 0, 0) + dot32(rz_a, a_v, 0, 0) + dot32(rz_d, d_v, 0, 0)
-        c_a = dot32(rz_a, e_a, 0, 0) + dot32(rz_d, d_a, 0, 0)
         c_d = dot32(rz_d, e_d, 0, 0)
+        c_v = c_v - dot32(c_d, d_v, 1, 0)
+        c_a = c_a - dot32(c_d, d_a, 1, 0)
         ch, cl = split(jnp.concatenate([c_v, c_d, c_a], axis=1))
         if it + 1 < ITERS:
             x = dot3(ch[0:K], cl[0:K], sh[...], sl[...], 1, 0)
@@ -523,8 +532,7 @@
             fd[...] = y
         else:
             new = dot3(ch, cl, sh[...], sl[...], 1, 0)
-            out_v[...] = new[0:K]
-            out_d[...] = new[K : 2 * K]
+            out[...] = new
 
     ref = tb.at[0, 0 : nz - 1]
     remote(ref, ref, tb_s.at[0], tb_r.at[0], sib).wait_send()
@@ -546,13 +554,12 @@
     prow = 96 // pieces
     calls = 1 + ITERS
     dma = pltpu.SemaphoreType.DMA
-    vmem, smem = pl.BlockSpec(memory_space=pltpu.VMEM), pl.BlockSpec(memory_space=pltpu.SMEM)
-    hbm = pl.BlockSpec(memory_space=pl.ANY)
-    return pl.pallas_call(
+    vmem, hbm = pl.BlockSpec(memory_space=pltpu.VMEM), pl.BlockSpec(memory_space=pl.ANY)
+    both = pl.pallas_call(
         functools.partial(kernel, ng, nz, width * ng * nr, slots),
-        out_shape=[jax.ShapeDtypeStruct(sv.shape, F32)] * 2,
-        in_specs=[hbm] * 5 + [smem] + [hbm] * 3,
-        out_specs=[vmem, vmem],
+        out_shape=jax.ShapeDtypeStruct((2 * K, width), F32),
+        in_specs=[hbm] * 9,
+        out_specs=vmem,
         scratch_shapes=[
             pltpu.VMEM((ITERS, far0 + 2 * ng, K, BS), BF16),
             pltpu.VMEM((ITERS, (nz - pos_a) * 2 * RB, K, BS), BF16),
@@ -571,18 +578,17 @@
             pltpu.VMEM((8, 128), I32),
             pltpu.VMEM((8, 128), I32),
             pltpu.SMEM((8, 128), I32),
-            pltpu.SMEM((128,), I32),
+            pltpu.SMEM((1,), I32),
             pltpu.SMEM(send_grp.shape, I32),
             pltpu.VMEM((8, 128), I32),
             pltpu.VMEM((2, nz, 8, 128), I32),
-            pltpu.VMEM((2 * nz, 128), I32),
-            pltpu.SMEM((2 * nz, 128), I32),
+            pltpu.VMEM((128, 128), I32),
             pltpu.VMEM((calls, 96, 128), F32),
             pltpu.VMEM((calls, 2 * ng, prow, 128), F32),
             pltpu.VMEM((calls, nz, prow, 128), F32),
             pltpu.VMEM((calls, 96, 128), F32),
             pltpu.VMEM((K, 2 * K), F32),
-            dma((10,)),
+            dma((11,)),
             dma((ITERS, 2)),
             dma((ITERS, 2, nz // 2, NCH)),
             dma((ITERS,)),
@@ -607,6 +613,7 @@
         sv, sd, tiles, tile_row.reshape(1, -1), tile_slot.reshape(1, -1), tile_count,
         send_row.reshape(1, -1), send_grp, ritz,
     )
+    return both[:K], both[K:]
 
 
 def solution(mesh):

time: 134 us -> 132 us (0.985)
  local copies, waits for them, and re-layouts: 3.34 us -> 1.87 us
    unnamed x2 -> x0, local copies, waits for them, and re-layouts: 3.34 us -> none
    slice x0 -> x1, local copies, waits for them, and re-layouts: none -> 1.87 us  [shards(): return (both[:K], both[K:])]
where the time goes in v3:
time: 132 us
  Pallas kernels  129 us (98%)
  local copies, waits for them, and re-layouts  1.87 us (1%)
    pallas_call x1, Pallas kernels, shards(): pl.pallas_call(functools.partial(kernel, ng, nz, width * ng * nr, slots),...  129 us

profile of v3, /device:TPU:1, one launch (start us, length us, event | category | flops | bytes accessed | tf_op | source)
XLA Modules:
  0.0 132.2 jit_solution(9242842667355395597)
XLA Ops:
  1.3 129.0 %shard_map.104 = f32[128,1024]{1,0:T(8,128)} custom-call(f32[64,1024]{1,0:T(8,128)} %sv.1, f32[64,1024]{1,0:T(8,128)} %sd.1, bf16[104,128,128]{2,1,0:T(8,128)(2,1)} %tiles.1, s32[1,104]{1,0:T(1,128)} %bitcast.3, s32[1,104]{1,0:T(1,128)} %bitcast.4, s32[1]{0:T(128)S(6)} %copy.11.count, s32[1,64]{1,0:T(1,128)} %bitcast.5, s32[32]{0:T(128)} %send_grp.1, ...), custom_call_target="tpu_custom_call" | custom-call | tf_op jit(solution)/shard_map/pallas_call | solution.py:558
  130.3 1.9 %fusion = (f32[64,1024]{1,0:T(8,128)}, f32[64,1024]{1,0:T(8,128)}) fusion(f32[128,1024]{1,0:T(8,128)} %shard_map.104), kind=kLoop, calls=%fused_computation | loop fusion | bytes 1048576 | tf_op jit(solution)/shard_map/slice | solution.py:616

commit v4 on v3

--- a/solution.py
+++ b/solution.py
@@ -441,15 +441,17 @@
         early = hops * 5 // 8 * NCH + 1
         ready = early - max(1, NCH // 2)
         last = (hops - 1) * NCH + NCH // 2
-        plan = [(0, functools.partial(send_far, it)), (1, functools.partial(get_directions, it))]
+        send_far(it)
+        get_directions(it)
+        plan = []
         if it == 0:
             mid = ready // 2 + 1
             tail = max(mid + 2, ready - 4)
+            send_table()
+            first_products()
+            order_tiles()
             plan += [
-                (0, send_table),
-                (2, first_products),
-                (2, functools.partial(sum_start, k0)),
-                (3, order_tiles),
+                (1, functools.partial(sum_start, k0)),
                 (mid, functools.partial(sum_plane, k0)),
                 (mid + 1, pass_table),
                 (tail, take_table),

time: 132 us -> 132 us (level)
  no operation moved by 1% of the time
where the time goes in v4:
time: 132 us
  Pallas kernels  129 us (98%)
  local copies, waits for them, and re-layouts  1.87 us (1%)
    pallas_call x1, Pallas kernels, shards(): pl.pallas_call(functools.partial(kernel, ng, nz, width * ng * nr, slots),...  129 us

profile of v4, /device:TPU:1, one launch (start us, length us, event | category | flops | bytes accessed | tf_op | source)
XLA Modules:
  0.0 131.9 jit_solution(5916594118403241929)
XLA Ops:
  1.3 128.8 %shard_map.104 = f32[128,1024]{1,0:T(8,128)} custom-call(f32[64,1024]{1,0:T(8,128)} %sv.1, f32[64,1024]{1,0:T(8,128)} %sd.1, bf16[104,128,128]{2,1,0:T(8,128)(2,1)} %tiles.1, s32[1,104]{1,0:T(1,128)} %bitcast.3, s32[1,104]{1,0:T(1,128)} %bitcast.4, s32[1]{0:T(128)S(6)} %copy.11.count, s32[1,64]{1,0:T(1,128)} %bitcast.5, s32[32]{0:T(128)} %send_grp.1, ...), custom_call_target="tpu_custom_call" | custom-call | tf_op jit(solution)/shard_map/pallas_call | solution.py:560
  130.0 1.9 %fusion = (f32[64,1024]{1,0:T(8,128)}, f32[64,1024]{1,0:T(8,128)}) fusion(f32[128,1024]{1,0:T(8,128)} %shard_map.104), kind=kLoop, calls=%fused_computation | loop fusion | bytes 1048576 | tf_op jit(solution)/shard_map/slice | solution.py:618
